TPU v7x, 256 devices: a whole 4x4x8 slice. The times are simulated.
256 devices in a mesh: tm: 32 (over z, y), clip: 8 (over x, core).
Axes of the slice: x: 4, y: 4, z: 8, core: 2. Of those that a mesh axis runs over, the one named last changes fastest.
Arguments:
- block_input: bfloat16 [8, 128, 16, 16, 256], P('clip', 'tm'), may hold values from -6 to 6
- pre_act: bfloat16 [8, 128, 16, 16, 512], P('clip', 'tm'), may hold values from -6 to 6
- time_out: bfloat16 [8, 128, 16, 16, 512], P('clip', 'tm'), may hold values from -6 to 6
- w_space: bfloat16 [256, 3, 3, 512], replicated, may hold values from -0.125 to 0.125
- w_time: bfloat16 [512, 3, 512], replicated, may hold values from -0.15625 to 0.15625
- proj: bfloat16 [512, 18], replicated, may hold values from -0.25 to 0.25
- codes: int32 [8, 128, 16, 16], P('clip', 'tm'), may hold values from 0 to 262143
- cotan: bfloat16 [8, 128, 16, 16, 18], P('clip', 'tm'), may hold values from -6 to 6
- lengths: int32 [8], replicated, may hold values from 1 to 128
Outputs:
- grad_input: bfloat16 [8, 128, 256, 256], P('clip', None, 'tm')
- grad_space: float32 [256, 3, 3, 512], P('tm')
- grad_time: float32 [512, 3, 512], P('tm')
- grad_proj: float32 [512, 18], P('tm')
All inputs are finite; a program needn't handle non-finite values.
Results may differ from a plain program's by a relative error of at most 0.025.
Values may be sent and summed in bfloat16 or wider, within the bound.
A program may use at most 64 MiB of HBM per device.

v0:
```python
import math

import jax
import jax.numpy as jnp
from jax import lax
from jax.sharding import PartitionSpec as P

commit_weight = 0.25


def from_behind(shard, axis, by):
    devices = lax.axis_size(axis)
    pairs = [(i, i + by) for i in range(devices) if 0 <= i + by < devices]
    return lax.ppermute(shard, axis, pairs)


def shift_space(values, down, right):
    side_len = values.shape[-2]
    padded = jnp.pad(values, ((0, 0), (1, 1), (1, 1), (0, 0)))
    return padded[:, 1 + down : 1 + down + side_len, 1 + right : 1 + right + side_len, :]


def silu_slope(pre):
    sigma = jax.nn.sigmoid(pre)
    return sigma * (1.0 + pre * (1.0 - sigma))


def sign_targets(flat_codes, latent):
    powers = (2 ** jnp.arange(latent)).astype(jnp.int32)
    bits = flat_codes[:, None] // powers[None, :] % 2
    return 2.0 * bits.astype(jnp.float32) - 1.0


def per_device(block_input, pre_act, time_out, w_space, w_time, proj, codes, cotan, lengths):
    clip_x = block_input[0]
    clip_pre = pre_act[0]
    frames_dev, side_len, _, cin = clip_x.shape
    cmid = clip_pre.shape[-1]
    latent = proj.shape[1]
    positions = side_len * side_len
    rows = frames_dev * positions
    slab_count = lax.axis_size("tm")
    group_count = lax.axis_size("clip")
    scale = 1.0 / math.sqrt(group_count * slab_count * rows)
    clip_len = lax.dynamic_index_in_dim(lengths, lax.axis_index("clip"), 0, keepdims=False)
    frame_ids = lax.axis_index("tm") * frames_dev + jnp.arange(frames_dev)
    live = (frame_ids < clip_len).astype(jnp.float32)
    live_rows = jnp.repeat(live, positions)[:, None]
    t_rows = time_out[0].reshape(rows, cmid)
    latent_z = jnp.dot(t_rows, proj, preferred_element_type=jnp.float32)
    targets = sign_targets(codes[0].reshape(rows), latent)
    grad_z = (
        live_rows
        * (
            cotan[0].reshape(rows, latent).astype(jnp.float32)
            + 2.0 * commit_weight * (latent_z - targets)
        )
    ).astype(jnp.bfloat16)
    proj_part = jnp.dot(t_rows.T, grad_z, preferred_element_type=jnp.float32)
    grad_t = jnp.dot(grad_z, proj.T, preferred_element_type=jnp.float32).astype(jnp.bfloat16)
    grad_t = grad_t.reshape(frames_dev, positions, cmid)
    grad_t_rows = grad_t.reshape(rows, cmid)
    next_frames = from_behind(grad_t[:2], "tm", -1)
    t_ext = jnp.concatenate([grad_t, next_frames], axis=0)
    act = (
        jax.nn.silu(clip_pre.astype(jnp.float32))
        .astype(jnp.bfloat16)
        .reshape(frames_dev, positions, cmid)
    )
    grad_act = jnp.zeros((rows, cmid), jnp.float32)
    for lag in range(3):
        ahead = t_ext[lag : lag + frames_dev].reshape(rows, cmid)
        grad_act = grad_act + jnp.dot(
            ahead, w_time[:, lag, :].T, preferred_element_type=jnp.float32
        )
    time_terms = []
    prev_frames = from_behind(act[frames_dev - 2 :], "tm", 1)
    a_ext = jnp.concatenate([prev_frames, act], axis=0)
    for lag in range(3):
        behind = a_ext[2 - lag : 2 - lag + frames_dev].reshape(rows, cmid)
        time_terms.append(jnp.dot(behind.T, grad_t_rows, preferred_element_type=jnp.float32))
    time_part = jnp.stack(time_terms, axis=1)
    grad_pre = (
        grad_act.reshape(frames_dev, side_len, side_len, cmid)
        * silu_slope(clip_pre.astype(jnp.float32))
    ).astype(jnp.bfloat16)
    pre_rows = grad_pre.reshape(rows, cmid)
    grad_x = jnp.zeros((frames_dev, side_len, side_len, cin), jnp.float32)
    space_rows = []
    for row_tap in range(3):
        row_terms = []
        for col_tap in range(3):
            moved = shift_space(clip_x, row_tap - 1, col_tap - 1).reshape(rows, cin)
            row_terms.append(jnp.dot(moved.T, pre_rows, preferred_element_type=jnp.float32))
            back = jnp.dot(
                pre_rows, w_space[:, row_tap, col_tap, :].T, preferred_element_type=jnp.float32
            )
            grad_x = grad_x + shift_space(
                back.reshape(frames_dev, side_len, side_len, cin), 1 - row_tap, 1 - col_tap
            )
        space_rows.append(jnp.stack(row_terms, axis=1))
    space_part = jnp.stack(space_rows, axis=1)
    grad_cells = grad_x.astype(jnp.bfloat16).reshape(1, frames_dev, positions, cin)
    grad_input = lax.all_to_all(grad_cells, "tm", split_axis=2, concat_axis=1, tiled=True)
    space_part = space_part * scale
    time_part = time_part * scale
    proj_part = proj_part * scale
    summed = (
        lax.psum(space_part.astype(jnp.bfloat16), "clip").astype(jnp.float32),
        lax.psum(time_part.astype(jnp.bfloat16), "clip").astype(jnp.float32),
        lax.psum(proj_part.astype(jnp.bfloat16), "clip").astype(jnp.float32),
    )
    owned = (
        lax.psum_scatter(
            summed[0].astype(jnp.bfloat16), "tm", scatter_dimension=0, tiled=True
        ).astype(jnp.float32),
        lax.psum_scatter(
            summed[1].astype(jnp.bfloat16), "tm", scatter_dimension=0, tiled=True
        ).astype(jnp.float32),
        lax.psum_scatter(
            summed[2].astype(jnp.bfloat16), "tm", scatter_dimension=0, tiled=True
        ).astype(jnp.float32),
    )
    return (grad_input, owned[0], owned[1], owned[2])


def solution(mesh):
    placed = (
        P("clip", "tm", None, None, None),
        P("clip", "tm", None, None, None),
        P("clip", "tm", None, None, None),
        P(),
        P(),
        P(),
        P("clip", "tm", None, None),
        P("clip", "tm", None, None, None),
        P(),
    )
    return jax.shard_map(
        per_device,
        mesh=mesh,
        in_specs=placed,
        out_specs=(
            P("clip", None, "tm", None),
            P("tm", None, None, None),
            P("tm", None, None),
            P("tm", None),
        ),
        check_vma=False,
    )
```

profile of v0, /device:TPU:1, one launch (start us, length us, event | category | flops | bytes accessed | tf_op | source)
XLA Modules:
  0.0 757.8 jit_solution(11394494174237194665)
XLA Ops:
  7.3 1.3 dynamic_slice.4
  9.3 0.8 broadcast_in_dim_reshape_squeeze.3
  10.1 1.0 bitcast_convert_fusion
  11.3 2.0 fusion.18
  13.9 1.3 collective-permute-start
  15.2 0.7 fusion.30
  15.9 11.3 %collective-permute-done = bf16[2,256,512]{2,1,0:T(8,128)(2,1)S(1)} collective-permute-done((bf16[2,256,512]{2,1,0:T(8,128)(2,1)S(1)}, bf16[2,256,512]{2,1,0:T(8,128)(2,1)S(1)}, u32[]{:S(2)}, u32[]{:S(2)}) %collective-permute-start) | collective-permute-done | bytes 524320 | tf_op jit(solution)/shard_map/ppermute | solution.py:14
  27.5 0.7 fusion.28
  28.7 2.5 fusion.9
  31.2 2.2 add_divide_fusion
  38.7 3.7 copy.45
  42.4 7.4 reshape.147
  50.1 0.8 copy.47
  51.1 1.7 convert_bitcast_fusion
  53.7 5.4 collective-permute-start.1
  59.1 0.7 convolution_bitcast_fusion.2
  59.8 2.4 fusion.35
  62.3 6.5 collective-permute-done.1
  69.6 0.7 convolution_bitcast_fusion.1
  70.4 1.6 fusion.1
  72.0 1.6 fusion.37
  76.9 0.8 fusion.14
  77.7 1.2 copy.22
  78.9 14.4 %all-to-all-start = ((bf16[1,4,256,256]{3,1,0,2:T(4,128)(2,1)}), bf16[1,4,256,256]{3,1,0,2:T(4,128)(2,1)S(1)}, u32[]{:S(2)}, u32[]{:S(2)}) async-start(bf16[1,4,256,256]{3,1,0,2:T(4,128)(2,1)} %copy.22), calls=%async_computation | async-start | bytes 1048576 | tf_op jit(solution)/shard_map/all_to_all | solution.py:104
  93.4 177.9 %reduce-scatter.10.cloned.1.call-done = bf16[8,4608]{1,0:T(8,128)(2,1)} async-done(((bf16[256,4608]{1,0:T(8,128)(2,1)}), bf16[8,4608]{1,0:T(8,128)(2,1)}) %reduce-scatter.10.cloned.1.call-update) | async-done | bytes 73744
  271.4 194.6 %reduce-scatter.12.cloned.1.call-done = bf16[16,18]{1,0:T(8,128)(2,1)} async-done(((bf16[512,18]{1,0:T(8,128)(2,1)}), bf16[16,18]{1,0:T(8,128)(2,1)}) %reduce-scatter.12.cloned.1.call-update) | async-done | bytes 592
  465.9 0.8 copy.48
  466.7 0.9 copy.23
  467.6 216.4 %reduce-scatter.8.cloned.1.call-done = bf16[16,3,512]{2,0,1:T(8,128)(2,1)} async-done(((bf16[512,3,512]{2,0,1:T(8,128)(2,1)}), bf16[16,3,512]{2,0,1:T(8,128)(2,1)}) %reduce-scatter.8.cloned.1.call-update) | async-done | bytes 49168 | tf_op jit(solution)/shard_map/reduce_scatter | solution.py:117
  684.0 27.6 %all-reduce.9 = (bf16[16,18]{0,1:T(8,128)(2,1)S(1)}, bf16[16,3,512]{2,0,1:T(8,128)(2,1)S(1)}) all-reduce(bf16[16,18]{0,1:T(8,128)(2,1)S(1)} %copy.48, bf16[16,3,512]{2,0,1:T(8,128)(2,1)} %reduce-scatter.8.cloned.1.call-done), channel_id=1, replica_groups=mesh['tm'=32,'clip'=8] {'clip'}, use_global_device_ids=true, to_apply=%region_4.5 | all-reduce | flops 24864 | bytes 99456 | tf_op jit(solution)/shard_map/psum | solution.py:111
  712.9 36.9 %all-reduce.12.cloned.1.call-done = bf16[8,3,3,512]{3,0,2,1:T(8,128)(2,1)} async-done(((bf16[8,3,3,512]{3,0,2,1:T(8,128)(2,1)}), bf16[8,3,3,512]{3,0,2,1:T(8,128)(2,1)}) %all-reduce.12.cloned.1.call-update) | async-done | bytes 73744 | tf_op jit(solution)/shard_map/psum | solution.py:109
  749.7 1.6 convert_element_type.117
  (64 shorter events, 14.3 us)
Async XLA Ops:
  7.2 4.2 copy-start
  7.2 6.2 copy-start.8
  7.2 264.1 %reduce-scatter.10.cloned.1.call-start = ((), (), s32[]{:S(2)}) async-start(), calls=%async_computation.6 | async-start | bytes 2433024
  11.3 3.9 copy-start.6
  13.9 13.4 %collective-permute-start = (bf16[2,256,512]{2,1,0:T(8,128)(2,1)S(1)}, bf16[2,256,512]{2,1,0:T(8,128)(2,1)S(1)}, u32[]{:S(2)}, u32[]{:S(2)}) collective-permute-start(bf16[2,256,512]{2,1,0:T(8,128)(2,1)S(1)} %bitcast.259), channel_id=1, source_target_pairs={{8,0},{16,8},{24,16},{32,24},{40,32},{48,40},{56,48},{64,56},{72,6... | collective-permute-start | bytes 1572872 | tf_op jit(solution)/shard_map/ppermute | solution.py:14
  27.5 1.2 copy-start.1
  31.2 2.2 copy-start.7
  49.8 416.2 %reduce-scatter.12.cloned.1.call-start = ((), (), s32[]{:S(2)}) async-start(), calls=%async_computation.7 | async-start | bytes 135168
  50.9 633.1 %reduce-scatter.8.cloned.1.call-start = ((), (), s32[]{:S(2)}) async-start(), calls=%async_computation.5 | async-start | bytes 1622016 | tf_op jit(solution)/shard_map/reduce_scatter | solution.py:117
  51.1 1.7 copy-start.2
  51.1 2.3 copy-start.3
  52.8 6.3 copy-start.9
  53.7 15.0 %collective-permute-start.1 = (bf16[2,256,512]{2,1,0:T(8,128)(2,1)S(1)}, bf16[2,256,512]{2,1,0:T(8,128)(2,1)S(1)}, u32[]{:S(2)}, u32[]{:S(2)}) collective-permute-start(bf16[2,256,512]{2,1,0:T(8,128)(2,1)S(1)} %bitcast.257), channel_id=1, source_target_pairs={{0,8},{8,16},{16,24},{24,32},{32,40},{40,48},{48,56},{56,64},{64,7... | collective-permute-start | bytes 1572872 | tf_op jit(solution)/shard_map/ppermute | solution.py:14
  72.0 1.7 copy-start.5
  75.7 1.2 copy-start.4
  78.9 387.8 %all-to-all-start = ((bf16[1,4,256,256]{3,1,0,2:T(4,128)(2,1)}), bf16[1,4,256,256]{3,1,0,2:T(4,128)(2,1)S(1)}, u32[]{:S(2)}, u32[]{:S(2)}) async-start(bf16[1,4,256,256]{3,1,0,2:T(4,128)(2,1)} %copy.22), calls=%async_computation | async-start | bytes 1048576 | tf_op jit(solution)/shard_map/all_to_all | solution.py:104
  93.4 656.3 %all-reduce.12.cloned.1.call-start = ((), (), s32[]{:S(2)}) async-start(), calls=%async_computation.4 | async-start | bytes 147456 | tf_op jit(solution)/shard_map/psum | solution.py:109
Sparse Core Ops, SparseCore 0:
  49.9 221.4 reduce-scatter.9
  275.5 190.3 reduce-scatter.11
  470.2 213.6 reduce-scatter.7
  686.3 63.3 all-reduce.11
where the time goes:
time: 759 us; the launch traced here: 758 us
  waiting for transfers between devices  644 us (85%)
  blocking collectives  27.6 us (4%)
  starting transfers between devices  21.4 us (3%)
  matrix products  20.7 us (3%)
  local copies, waits for them, and re-layouts  18.8 us (2%)
  between operations  14.2 us (2%)
  other arithmetic  11.6 us (2%)
    unnamed x6, waiting for transfers between devices  373 us
    reduce_scatter x1, waiting for transfers between devices, per_device(): lax.psum_scatter(summed[1].astype(jnp.bfloat16), 'tm', scatter_dimension=...  216 us
    psum x1, waiting for transfers between devices, per_device(): lax.psum(space_part.astype(jnp.bfloat16), 'clip').astype(jnp.float32)  36.9 us
    psum x1, blocking collectives, per_device(): lax.psum(proj_part.astype(jnp.bfloat16), 'clip').astype(jnp.float32)  27.6 us
    ppermute x2, waiting for transfers between devices, from_behind(): return lax.ppermute(shard, axis, pairs)  17.8 us
  transfers between devices with their start and end apart: 7, of which 6 were waited for; matrix products, arithmetic and copies ran while one was open for 3% of the time, Pallas kernels for 0%

commit v1 on v0

v1 whole, which is shorter than its diff:
```python
import jax
import jax.numpy as jnp
from jax import lax
from jax.experimental import pallas as pl
from jax.experimental.pallas import tpu as pltpu
from jax.sharding import PartitionSpec as P

MESH = pl.DeviceIdType.MESH
F32 = jnp.float32
BF16 = jnp.bfloat16
I32 = jnp.int32

NZ, NY, NX, NC = 8, 4, 4, 2
NT, NG = NZ * NY, NX * NC
FR, CELLS, CIN, CMID, LAT = 4, 256, 256, 512, 18
ROWS = FR * CELLS
PAIR = 2 * CELLS
SCALE = 1.0 / 512.0

NT_DIMS = (((1,), (1,)), ((), ()))
TN_DIMS = (((0,), (0,)), ((), ()))


def iota(shape, dim):
    return lax.broadcasted_iota(I32, shape, dim)


def ones_where(cond):
    return jnp.where(cond, 1.0, 0.0).astype(BF16)


def dot(a, b):
    return jnp.dot(a, b, preferred_element_type=F32)


def dot_nt(a, b):
    return lax.dot_general(a, b, NT_DIMS, preferred_element_type=F32)


def dot_tn(a, b):
    return lax.dot_general(a, b, TN_DIMS, preferred_element_type=F32)


def kernel(
    x_hbm, pre_hbm, t_hbm, ws_hbm, wt_hbm, pj_hbm, codes_hbm, cot_hbm, len_ref,
    out_hbm, space_ref, time_ref, proj_ref,
    x_v, pre_v, t_v, ws_v, wt_v, pj_v, codes_v, cot_v,
    p3_v, gz_v, zc_v, mt_v, act_v, slope_v, g3_v, xt_v,
    halo_s, halo_r, ab_v,
    pw1, pw2, rc1, rc2,
    rel1, rel2, sum1, sum2, fin1, fin2,
    yb, ry, zs, rz, fs, ra,
    in_sem, halo_ss, halo_rs, a2a_ss, a2a_rs,
    core_ss, core_rs, x_ss, x_rs, y_ss, y_rs, z_ss, z_rs, g_ss, g_rs,
):
    tm = lax.axis_index("tm")
    clip = lax.axis_index("clip")
    z, y = tm // NY, tm % NY
    x, core = clip // NC, clip % NC

    def load(src, dst, i):
        copy = pltpu.make_async_copy(src, dst, in_sem.at[i])
        copy.start()
        return copy

    ld_pj = load(pj_hbm, pj_v, 0)
    ld_t0 = load(t_hbm.at[pl.ds(0, PAIR)], t_v.at[pl.ds(0, PAIR)], 1)
    ld_cd = load(codes_hbm, codes_v, 2)
    ld_ct = load(cot_hbm, cot_v, 3)
    ld_t1 = load(t_hbm.at[pl.ds(PAIR, PAIR)], t_v.at[pl.ds(PAIR, PAIR)], 4)
    ld_wt = load(wt_hbm, wt_v, 5)
    ld_pre = load(pre_hbm, pre_v, 6)
    ld_x = load(x_hbm, x_v, 7)
    ld_ws = load(ws_hbm, ws_v, 8)

    barrier = pltpu.get_barrier_semaphore()

    @pl.loop(1, NT)
    def _(d):
        pl.semaphore_signal(
            barrier, inc=1, device_id=(lax.rem(tm + d, NT), clip), device_id_type=MESH
        )

    @pl.loop(1, NG)
    def _(d):
        pl.semaphore_signal(
            barrier, inc=1, device_id=(tm, lax.rem(clip + d, NG)), device_id_type=MESH
        )

    ld_pj.wait()
    row_l = iota((128, LAT), 0) % 32
    rep = ones_where(row_l == iota((128, LAT), 1))
    p3_v[...] = dot(rep, pj_v[...]).astype(BF16)

    rep_t = ones_where(iota((LAT, 128), 0) == iota((LAT, 128), 1) % 32)
    lane = iota((PAIR, 128), 1)
    lane_l = lane % 32
    row_id = iota((PAIR, 128), 0)
    spread = ones_where(iota((PAIR, 32), 0) // 16 == iota((PAIR, 32), 1))
    pick = ones_where(
        (iota((128, 128), 0) // 16 == (iota((128, 128), 1) % 32) // 6)
        & (iota((128, 128), 1) % 32 < LAT)
    )
    clip_len = len_ref[clip]

    def latents(fp):
        rows = pl.ds(fp * PAIR, PAIR)
        lat = dot_nt(t_v[rows, :], p3_v[...])
        cot = dot(cot_v[rows, :], rep_t)
        cd = codes_v[pl.ds(fp * 32, 32), :]
        packed = jnp.zeros((32, 128), F32)
        for piece in range(3):
            part = ((cd >> (6 * piece)) & 63).astype(F32).astype(BF16)
            place = ones_where(iota((16, 128), 1) == iota((16, 128), 0) + 16 * piece)
            packed = packed + dot(part, place)
        wide = dot(spread, packed.astype(BF16))
        own = jnp.where((lane < 48) & (lane % 16 == row_id % 16), wide, 0.0)
        six = dot(own.astype(BF16), pick).astype(I32)
        bit = (six >> (lane_l % 6)) & 1
        target = (2 * bit - 1).astype(F32)
        frame = tm * FR + fp * 2 + row_id // CELLS
        keep = (frame < clip_len) & (lane_l < LAT)
        grad = jnp.where(keep, cot + 0.5 * (lat - target), 0.0)
        gz_v[rows, :] = grad.astype(BF16)

    ld_t0.wait()
    ld_cd.wait()
    ld_ct.wait()
    latents(0)

    group = iota((CELLS, 128), 1) // 32

    def gz(f):
        return gz_v[f * CELLS : (f + 1) * CELLS, :].astype(F32)

    halo_s[...] = jnp.where(
        group == 0, 0.0, jnp.where(group == 2, gz(1), gz(0))
    ).astype(BF16)
    pl.semaphore_wait(barrier, NT - 1 + NG - 1)
    halo = pltpu.make_async_remote_copy(
        src_ref=halo_s, dst_ref=halo_r, send_sem=halo_ss, recv_sem=halo_rs,
        device_id=(lax.rem(tm + NT - 1, NT), clip), device_id_type=MESH,
    )
    halo.start()

    ld_t1.wait()
    latents(1)
    zc_v[0:CELLS, :] = jnp.where(
        group == 0, gz(0), jnp.where(group == 1, gz(1), jnp.where(group == 2, gz(2), 0.0))
    ).astype(BF16)
    zc_v[CELLS:PAIR, :] = jnp.where(
        group == 0, gz(1), jnp.where(group == 1, gz(2), jnp.where(group == 2, gz(3), 0.0))
    ).astype(BF16)

    ld_wt.wait()
    for k in range(3):
        folded = dot_nt(p3_v[0:32, :], wt_v[k]).astype(BF16)
        mt_v[32 * k : 32 * k + 32, :] = folded
        if k == 2:
            mt_v[96:128, :] = folded

    ld_pre.wait()

    @pl.loop(0, ROWS // 64)
    def _(i):
        rows = pl.ds(pl.multiple_of(i * 64, 64), 64)
        v = pre_v[rows, :].astype(F32)
        s = 0.5 * jnp.tanh(0.5 * v) + 0.5
        a = v * s
        act_v[rows, :] = a.astype(BF16)
        slope_v[rows, :] = s + a * (1.0 - s)

    zero16 = jnp.zeros((16, CMID), BF16)

    def grad_pre(f):
        lo, hi = f * CELLS, (f + 1) * CELLS
        g = (dot(zc_v[lo:hi, :], mt_v[...]) * slope_v[lo:hi, :]).astype(BF16)
        g3_v[1, lo:hi, :] = g
        g3_v[0, lo : hi - 16, :] = g[16:]
        g3_v[0, hi - 16 : hi, :] = zero16
        g3_v[2, lo + 16 : hi, :] = g[: CELLS - 16]
        g3_v[2, lo : lo + 16, :] = zero16

    row_p = iota((PAIR, CIN), 0) % 16

    def grad_x(fp):
        rows = slice(fp * PAIR, (fp + 1) * PAIR)
        back = []
        for b in range(3):
            acc = dot_nt(g3_v[0, rows, :], ws_v[b])
            for a in range(1, 3):
                acc = acc + dot_nt(g3_v[a, rows, :], ws_v[3 * a + b])
            back.append(acc)
        g = (
            back[1]
            + jnp.where(row_p != 15, pltpu.roll(back[0], PAIR - 1, 0), 0.0)
            + jnp.where(row_p != 0, pltpu.roll(back[2], 1, 0), 0.0)
        )
        for t in range(NT):
            both = jnp.concatenate(
                [g[8 * t : 8 * t + 8], g[CELLS + 8 * t : CELLS + 8 * t + 8]], axis=0
            )
            ab_v[t, fp] = both.astype(BF16)

        @pl.loop(1, NT)
        def _(d):
            to = lax.rem(tm + d, NT)
            pltpu.make_async_remote_copy(
                src_ref=ab_v.at[to, fp], dst_ref=out_hbm.at[2 * tm + fp],
                send_sem=a2a_ss, recv_sem=a2a_rs,
                device_id=(to, clip), device_id_type=MESH,
            ).start()

        pltpu.make_async_copy(ab_v.at[tm, fp], out_hbm.at[2 * tm + fp], a2a_rs).start()

    grad_pre(0)
    grad_pre(1)
    ld_ws.wait()
    grad_x(0)

    ld_x.wait()
    r = iota((CIN, CIN), 0)
    c = iota((CIN, CIN), 1)
    perm = ones_where(
        c == (r // 16) % 4 * 64 + (r // 8) % 2 * 32 + r // 64 * 8 + r % 8
    )
    shift_lo = ones_where((r == c - 1) & (c % 16 != 0))
    shift_hi = ones_where((r == c + 1) & (c % 16 != 15))
    for f in range(FR):
        lo, hi = f * CELLS, (f + 1) * CELLS
        xt = dot_nt(perm, x_v[lo:hi, :]).astype(BF16)
        xt_v[256:512, lo:hi] = xt
        xt_v[0:256, lo:hi] = dot(xt, shift_lo).astype(BF16)
        xt_v[512:768, lo:hi] = dot(xt, shift_hi).astype(BF16)

    halo.wait_recv()
    ahead = jnp.where(tm == NT - 1, 0.0, halo_r[...].astype(F32))
    zc_v[PAIR : PAIR + CELLS, :] = jnp.where(
        group == 0, gz(2), jnp.where(group == 1, gz(3), jnp.where(group == 3, ahead, 0.0))
    ).astype(BF16)
    zc_v[PAIR + CELLS :, :] = jnp.where(
        group == 0, gz(3), jnp.where(group == 3, 0.0, ahead)
    ).astype(BF16)
    grad_pre(2)
    grad_pre(3)

    gt = dot_tn(zc_v[...], act_v[...])
    pt = dot_tn(gz_v[...], t_v[...])
    q_t = jnp.concatenate([gt[0:64], gt[64:96] + gt[96:128], pt[96:128]], axis=0)
    q = q_t.T
    for cc in range(NC):
        for yy in range(NY):
            for zp in range(NZ // 2):
                lo = 16 * (2 * zp * NY + yy) + 8 * cc
                hi = 16 * ((2 * zp + 1) * NY + yy) + 8 * cc
                tile = jnp.concatenate([q[lo : lo + 8], q[hi : hi + 8]], axis=0).astype(BF16)
                at = yy * 64 + zp * 16
                pw2[cc, 3, 0, at : at + 16, :] = tile
                pw2[cc, 3, 1, at : at + 16, :] = tile

    def space(a, half):
        cols = pl.ds(pl.multiple_of(half * 256, 256), 256)
        acc = dot(xt_v[...], g3_v[a, :, cols])
        for b in range(3):
            for lb in range(2):
                block = acc[256 * b : 256 * b + 256, 128 * lb : 128 * lb + 128].astype(BF16)
                if a < 2:
                    i = 6 * a + 2 * b + lb
                    pw1[half, i // 3, i % 3] = block
                else:
                    i = 2 * b + lb
                    pw2[half, i // 2, i % 2] = block

    other = 1 - core
    mate = (tm, x * NC + other)

    def core_copy(src, dst, i):
        return pltpu.make_async_remote_copy(
            src_ref=src, dst_ref=dst, send_sem=core_ss.at[i], recv_sem=core_rs.at[i],
            device_id=mate, device_id_type=MESH,
        )

    core_copies = (
        core_copy(pw1.at[other, pl.ds(0, 2)], rc1.at[pl.ds(0, 2)], 0),
        core_copy(pw1.at[other, pl.ds(2, 2)], rc1.at[pl.ds(2, 2)], 1),
        core_copy(pw2.at[other], rc2, 2),
    )
    for a in range(3):
        space(a, other)
        core_copies[a].start()
    for a in range(3):
        space(a, core)

    left, right, far = lax.rem(x + 3, NX), lax.rem(x + 1, NX), lax.rem(x + 2, NX)

    def x_copy(src, dst, to, i):
        return pltpu.make_async_remote_copy(
            src_ref=src, dst_ref=dst, send_sem=x_ss.at[i], recv_sem=x_rs.at[i],
            device_id=(tm, to * NC + core), device_id_type=MESH,
        )

    half_a, half_b = pl.ds(0, 128), pl.ds(128, 128)

    def x_first(w, pw, rc, rel, sm, fin):
        def add(chunk):
            for s in range(pw.shape[2]):
                sm[chunk, s] = (pw[core, chunk, s].astype(F32) + rc[chunk, s].astype(F32)).astype(BF16)

        add(far)
        to_l = x_copy(sm.at[far, :, half_a], rel.at[0], left, w + 0)
        to_r = x_copy(sm.at[far, :, half_b], rel.at[1], right, w + 1)
        to_l.start()
        to_r.start()
        add(left)
        d_l = x_copy(sm.at[left, :, half_b], fin.at[1, :, half_b], left, w + 2)
        d_l.start()
        add(right)
        d_r = x_copy(sm.at[right, :, half_a], fin.at[0, :, half_a], right, w + 3)
        d_r.start()
        add(x)
        return [to_l, to_r, d_l, d_r]

    def x_second(w, rel, sm, fin, copies):
        n = sm.shape[1]
        copies[0].wait_recv()
        for s in range(n):
            sm[left, s, 0:128] = (sm[left, s, 0:128].astype(F32) + rel[0, s].astype(F32)).astype(BF16)
        s_l = x_copy(sm.at[left, :, half_a], fin.at[1, :, half_a], left, w + 4)
        s_l.start()
        copies[1].wait_recv()
        for s in range(n):
            sm[right, s, 128:256] = (sm[right, s, 128:256].astype(F32) + rel[1, s].astype(F32)).astype(BF16)
        s_r = x_copy(sm.at[right, :, half_b], fin.at[0, :, half_b], right, w + 5)
        s_r.start()
        return [s_l, s_r]

    core_copies[0].wait_recv()
    core_copies[1].wait_recv()
    first1 = x_first(0, pw1, rc1, rel1, sum1, fin1)
    core_copies[2].wait_recv()
    first2 = x_first(6, pw2, rc2, rel2, sum2, fin2)

    grad_x(1)

    second1 = x_second(0, rel1, sum1, fin1, first1)
    second2 = x_second(6, rel2, sum2, fin2, first2)

    def x_last(sm, fin, first, second, base):
        for copy in first[2:] + second:
            copy.wait_recv()
        for s in range(sm.shape[1]):
            tot = sm[x, s].astype(F32) + fin[0, s].astype(F32) + fin[1, s].astype(F32)
            tot = tot.astype(BF16)
            for yy in range(NY):
                yb[yy, base + s] = tot[64 * yy : 64 * yy + 64]

    x_last(sum1, fin1, first1, second1, 0)
    x_last(sum2, fin2, first2, second2, 3)

    y_copies = []
    for d in range(1, NY):
        to = lax.rem(y + d, NY)
        copy = pltpu.make_async_remote_copy(
            src_ref=yb.at[to], dst_ref=ry.at[d - 1],
            send_sem=y_ss.at[d - 1], recv_sem=y_rs.at[d - 1],
            device_id=(z * NY + to, clip), device_id_type=MESH,
        )
        copy.start()
        y_copies.append(copy)
    for copy in y_copies:
        copy.wait_recv()
    tots = []
    for s in range(5):
        tot = yb[y, s].astype(F32)
        for d in range(NY - 1):
            tot = tot + ry[d, s].astype(F32)
        tots.append(tot)
    blank = jnp.zeros((8, 128), F32)
    for zz in range(NZ):
        eights = [tot[8 * zz : 8 * zz + 8] for tot in tots] + [blank]
        for i in range(3):
            zs[zz, 16 * i : 16 * i + 16] = jnp.concatenate(
                eights[2 * i : 2 * i + 2], axis=0
            ).astype(BF16)

    z_copies = []
    for d in range(1, NZ):
        to = lax.rem(z + d, NZ)
        copy = pltpu.make_async_remote_copy(
            src_ref=zs.at[to], dst_ref=rz.at[d - 1],
            send_sem=z_ss.at[d - 1], recv_sem=z_rs.at[d - 1],
            device_id=(to * NY + y, clip), device_id_type=MESH,
        )
        copy.start()
        z_copies.append(copy)
    for copy in z_copies:
        copy.wait_recv()
    tot = zs[z].astype(F32)
    for d in range(NZ - 1):
        tot = tot + rz[d].astype(F32)
    fs[...] = (tot * SCALE).astype(BF16)
    ra[clip] = fs[...]

    g_copies = []
    for d in range(1, NG):
        copy = pltpu.make_async_remote_copy(
            src_ref=fs, dst_ref=ra.at[clip],
            send_sem=g_ss.at[d - 1], recv_sem=g_rs.at[d - 1],
            device_id=(tm, lax.rem(clip + d, NG)), device_id_type=MESH,
        )
        copy.start()
        g_copies.append(copy)
    for copy in g_copies:
        copy.wait_recv()

    for cc in range(NC):
        for i in range(18):
            a, b, lb = i // 6, i // 2 % 3, i % 2
            if a < 2:
                xx, s = i // 3, i % 3
            else:
                xx, s = (i - 12) // 2, 3 + i % 2
            tile = ra[xx * NC + cc, 16 * (s // 2) : 16 * (s // 2) + 16].astype(F32)
            lo = 256 * cc + 128 * lb
            space_ref[3 * a + b, :, lo : lo + 128] = tile[8 * (s % 2) : 8 * (s % 2) + 8]
    qs = jnp.concatenate([ra[3 * NC + cc, 16:32].astype(F32)[8:16] for cc in range(NC)], axis=0)
    q_lane = iota((16, 128), 1)
    for k in range(3):
        time_ref[k] = dot(jnp.where(q_lane // 32 == k, qs, 0.0).astype(BF16), p3_v[...])
    take = ones_where(iota((128, LAT), 0) == iota((128, LAT), 1) + 96)
    proj_ref[...] = dot(qs.astype(BF16), take)

    halo.wait_send()
    for copy in core_copies:
        copy.wait_send()
    for copy in first1 + first2 + second1 + second2 + y_copies + z_copies + g_copies:
        copy.wait_send()
    sent = ab_v.at[pl.ds(0, NT - 1)]
    pltpu.make_async_copy(sent, sent, a2a_ss).wait()
    pltpu.make_async_copy(out_hbm, out_hbm, a2a_rs).wait()


def per_device(block_input, pre_act, time_out, w_space, w_time, proj, codes, cotan, lengths):
    args = (
        block_input.reshape(ROWS, CIN),
        pre_act.reshape(ROWS, CMID),
        time_out.reshape(ROWS, CMID),
        w_space.transpose(1, 2, 0, 3).reshape(9, CIN, CMID),
        w_time.transpose(1, 0, 2),
        proj.T,
        codes.reshape(FR * 16, 16),
        cotan.reshape(ROWS, LAT),
        lengths,
    )
    anywhere = pl.BlockSpec(memory_space=pl.ANY)
    vmem = pl.BlockSpec(memory_space=pltpu.VMEM)
    dma = pltpu.SemaphoreType.DMA
    v = pltpu.VMEM
    out, space, time, projg = pl.pallas_call(
        kernel,
        out_shape=(
            jax.ShapeDtypeStruct((2 * NT, 16, CIN), BF16),
            jax.ShapeDtypeStruct((9, 8, CMID), F32),
            jax.ShapeDtypeStruct((3, 16, CMID), F32),
            jax.ShapeDtypeStruct((16, LAT), F32),
        ),
        in_specs=[anywhere] * 8 + [pl.BlockSpec(memory_space=pltpu.SMEM)],
        out_specs=(anywhere, vmem, vmem, vmem),
        scratch_shapes=[
            v((ROWS, CIN), BF16), v((ROWS, CMID), BF16), v((ROWS, CMID), BF16),
            v((9, CIN, CMID), BF16), v((3, CMID, CMID), BF16), v((LAT, CMID), BF16),
            v((FR * 16, 16), I32), v((ROWS, LAT), BF16),
            v((128, CMID), BF16), v((ROWS, 128), BF16), v((ROWS, 128), BF16),
            v((128, CMID), BF16), v((ROWS, CMID), BF16), v((ROWS, CMID), F32),
            v((3, ROWS, CMID), BF16), v((768, ROWS), BF16),
            v((CELLS, 128), BF16), v((CELLS, 128), BF16), v((NT, 2, 16, CIN), BF16),
            v((NC, NX, 3, 256, 128), BF16), v((NC, NX, 2, 256, 128), BF16),
            v((NX, 3, 256, 128), BF16), v((NX, 2, 256, 128), BF16),
            v((2, 3, 128, 128), BF16), v((2, 2, 128, 128), BF16),
            v((NX, 3, 256, 128), BF16), v((NX, 2, 256, 128), BF16),
            v((2, 3, 256, 128), BF16), v((2, 2, 256, 128), BF16),
            v((NY, 5, 64, 128), BF16), v((NY - 1, 5, 64, 128), BF16),
            v((NZ, 48, 128), BF16), v((NZ - 1, 48, 128), BF16),
            v((48, 128), BF16), v((NG, 48, 128), BF16),
            dma((9,)), dma(()), dma(()), dma(()), dma(()),
            dma((3,)), dma((3,)), dma((12,)), dma((12,)),
            dma((NY - 1,)), dma((NY - 1,)), dma((NZ - 1,)), dma((NZ - 1,)),
            dma((NG - 1,)), dma((NG - 1,)),
        ],
        compiler_params=pltpu.CompilerParams(
            collective_id=0, has_side_effects=True, vmem_limit_bytes=56 * 1024 * 1024
        ),
    )(*args)
    return (
        out.reshape(1, FR * NT, 8, CIN),
        space.reshape(3, 3, 8, CMID).transpose(2, 0, 1, 3),
        time.transpose(1, 0, 2),
        projg,
    )


def solution(mesh):
    placed = (
        P("clip", "tm", None, None, None),
        P("clip", "tm", None, None, None),
        P("clip", "tm", None, None, None),
        P(),
        P(),
        P(),
        P("clip", "tm", None, None),
        P("clip", "tm", None, None, None),
        P(),
    )
    return jax.shard_map(
        per_device,
        mesh=mesh,
        in_specs=placed,
        out_specs=(
            P("clip", None, "tm", None),
            P("tm", None, None, None),
            P("tm", None, None),
            P("tm", None),
        ),
        check_vma=False,
    )
```

time: 759 us -> 57.6 us (0.08)
  waiting for transfers between devices: 644 us -> 0 us
  Pallas kernels: 0 us -> 50.4 us
  blocking collectives: 27.6 us -> 0 us
  starting transfers between devices: 21.4 us -> 0 us
  matrix products: 20.7 us -> 0 us
  between operations: 14.2 us -> 0.64 us
  local copies, waits for them, and re-layouts: 18.8 us -> 6.28 us
  other arithmetic: 11.6 us -> 0 us
    unnamed x6 -> x0, waiting for transfers between devices: 373 us -> none
    reduce_scatter x1 -> x0, waiting for transfers between devices: 216 us -> none  [per_device(): lax.psum_scatter(summed[1].astype(jnp.bfloat16), 'tm', scatter_dimension=...]
    pallas_call x0 -> x1, Pallas kernels: none -> 50.4 us  [per_device(): pl.pallas_call(kernel, out_shape=(jax.ShapeDtypeStruct((2 * NT, 16, CIN),...]
    psum x1 -> x0, waiting for transfers between devices: 36.9 us -> none  [per_device(): lax.psum(space_part.astype(jnp.bfloat16), 'clip').astype(jnp.float32)]
    psum x1 -> x0, blocking collectives: 27.6 us -> none  [per_device(): lax.psum(proj_part.astype(jnp.bfloat16), 'clip').astype(jnp.float32)]
    dot_general x27 -> x0, matrix products: 20.7 us -> none  [the longest x9 7.6 us: per_device(): jnp.dot(pre_rows, w_space[:, row_tap, col_tap, :].T, preferred_element_ty...]
    ppermute x2 -> x0, waiting for transfers between devices: 17.8 us -> none  [from_behind(): return lax.ppermute(shard, axis, pairs)]
    all_to_all x1 -> x0, starting transfers between devices: 14.4 us -> none  [per_device(): lax.all_to_all(grad_cells, 'tm', split_axis=2, concat_axis=1, tiled=True)]
  transfers between devices with their start and end apart: 7 -> 0, of which waited for: 6 -> 0; matrix products, arithmetic and copies ran while one was open for 3% -> 0% of each run, Pallas kernels for 0% -> 0%
where the time goes in v1:
time: 57.6 us; the launch traced here: 57.3 us
  Pallas kernels  50.4 us (88%)
  local copies, waits for them, and re-layouts  6.28 us (11%)
  between operations  0.64 us (1%)
    pallas_call x1, Pallas kernels, per_device(): pl.pallas_call(kernel, out_shape=(jax.ShapeDtypeStruct((2 * NT, 16, CIN),...  50.4 us
    unnamed x4, local copies, waits for them, and re-layouts  6.28 us

profile of v1, /device:TPU:1, one launch (start us, length us, event | category | flops | bytes accessed | tf_op | source)
XLA Modules:
  0.0 57.3 jit_solution(11747394661403486571)
XLA Ops:
  0.6 50.4 %shard_map.120 = (bf16[64,16,256]{2,1,0:T(8,128)(2,1)}, f32[9,8,512]{2,1,0:T(8,128)}, f32[3,16,512]{2,1,0:T(8,128)}, f32[16,18]{1,0:T(8,128)}) custom-call(bf16[1024,256]{1,0:T(8,128)(2,1)} %bitcast.20, bf16[1024,512]{1,0:T(8,128)(2,1)} %bitcast.17, bf16[1024,512]{1,0:T(8,128)(2,1)} %bitcast.18, bf16[9,256,512]{2,1,0:T(8,128)(2,1)} %bitcast.15, ...), custom_call_target="tpu_custom_call" | custom-call | tf_op jit(solution)/shard_map/pallas_call | solution.py:459
  51.0 1.9 %copy.17 = bf16[1,128,8,256]{3,2,1,0:T(8,128)(2,1)} copy(bf16[1,128,8,256]{3,2,1,0:T(8,128)(2,1)} %bitcast.19) | data formatting | bytes 1048576
  52.9 1.6 %copy.18 = f32[8,3,3,512]{3,0,2,1:T(8,128)} copy(f32[8,3,3,512]{3,0,2,1:T(8,128)} %bitcast.22) | data formatting | bytes 294912
  54.5 1.5 %copy.19 = f32[16,3,512]{2,0,1:T(8,128)} copy(f32[16,3,512]{2,0,1:T(8,128)} %bitcast.23) | data formatting | bytes 196608
  56.0 1.3 %copy.20 = f32[16,18]{1,0:T(8,128)} copy(f32[16,18]{1,0:T(8,128)} %get-tuple-element.19) | data formatting | bytes 2304

commit v2 on v1

--- a/solution.py
+++ b/solution.py
@@ -42,14 +42,14 @@
 
 
 def kernel(
-    x_hbm, pre_hbm, t_hbm, ws_hbm, wt_hbm, pj_hbm, codes_hbm, cot_hbm, len_ref,
-    out_hbm, space_ref, time_ref, proj_ref,
-    x_v, pre_v, t_v, ws_v, wt_v, pj_v, codes_v, cot_v,
+    x_hbm, pre_hbm, t_hbm, ws_hbm, wt_hbm, pj_hbm, codes_hbm, cot_hbm, len_hbm,
+    out_hbm, ra,
+    x_v, pre_v, t_v, ws_v, wt_v, pj_v, codes_v, cot_v, len_ref,
     p3_v, gz_v, zc_v, mt_v, act_v, slope_v, g3_v, xt_v,
     halo_s, halo_r, ab_v,
     pw1, pw2, rc1, rc2,
     rel1, rel2, sum1, sum2, fin1, fin2,
-    yb, ry, zs, rz, fs, ra,
+    last1, last2, got1, got2, zs, rz,
     in_sem, halo_ss, halo_rs, a2a_ss, a2a_rs,
     core_ss, core_rs, x_ss, x_rs, y_ss, y_rs, z_ss, z_rs, g_ss, g_rs,
 ):
@@ -67,6 +67,7 @@
     ld_t0 = load(t_hbm.at[pl.ds(0, PAIR)], t_v.at[pl.ds(0, PAIR)], 1)
     ld_cd = load(codes_hbm, codes_v, 2)
     ld_ct = load(cot_hbm, cot_v, 3)
+    ld_len = load(len_hbm, len_ref, 9)
     ld_t1 = load(t_hbm.at[pl.ds(PAIR, PAIR)], t_v.at[pl.ds(PAIR, PAIR)], 4)
     ld_wt = load(wt_hbm, wt_v, 5)
     ld_pre = load(pre_hbm, pre_v, 6)
@@ -101,6 +102,7 @@
         (iota((128, 128), 0) // 16 == (iota((128, 128), 1) % 32) // 6)
         & (iota((128, 128), 1) % 32 < LAT)
     )
+    ld_len.wait()
     clip_len = len_ref[clip]
 
     def latents(fp):
@@ -153,11 +155,11 @@
     ).astype(BF16)
 
     ld_wt.wait()
-    for k in range(3):
-        folded = dot_nt(p3_v[0:32, :], wt_v[k]).astype(BF16)
-        mt_v[32 * k : 32 * k + 32, :] = folded
-        if k == 2:
-            mt_v[96:128, :] = folded
+    lane_g = iota((CMID, 128), 1) // 32
+    fold = dot_nt(wt_v[2], p3_v[...])
+    for k in range(2):
+        fold = jnp.where(lane_g == k, dot_nt(wt_v[k], p3_v[...]), fold)
+    mt_v[...] = fold.astype(BF16)
 
     ld_pre.wait()
 
@@ -174,7 +176,7 @@
 
     def grad_pre(f):
         lo, hi = f * CELLS, (f + 1) * CELLS
-        g = (dot(zc_v[lo:hi, :], mt_v[...]) * slope_v[lo:hi, :]).astype(BF16)
+        g = (dot_nt(zc_v[lo:hi, :], mt_v[...]) * slope_v[lo:hi, :]).astype(BF16)
         g3_v[1, lo:hi, :] = g
         g3_v[0, lo : hi - 16, :] = g[16:]
         g3_v[0, hi - 16 : hi, :] = zero16
@@ -215,8 +217,6 @@
 
     grad_pre(0)
     grad_pre(1)
-    ld_ws.wait()
-    grad_x(0)
 
     ld_x.wait()
     r = iota((CIN, CIN), 0)
@@ -244,20 +244,6 @@
     grad_pre(2)
     grad_pre(3)
 
-    gt = dot_tn(zc_v[...], act_v[...])
-    pt = dot_tn(gz_v[...], t_v[...])
-    q_t = jnp.concatenate([gt[0:64], gt[64:96] + gt[96:128], pt[96:128]], axis=0)
-    q = q_t.T
-    for cc in range(NC):
-        for yy in range(NY):
-            for zp in range(NZ // 2):
-                lo = 16 * (2 * zp * NY + yy) + 8 * cc
-                hi = 16 * ((2 * zp + 1) * NY + yy) + 8 * cc
-                tile = jnp.concatenate([q[lo : lo + 8], q[hi : hi + 8]], axis=0).astype(BF16)
-                at = yy * 64 + zp * 16
-                pw2[cc, 3, 0, at : at + 16, :] = tile
-                pw2[cc, 3, 1, at : at + 16, :] = tile
-
     def space(a, half):
         cols = pl.ds(pl.multiple_of(half * 256, 256), 256)
         acc = dot(xt_v[...], g3_v[a, :, cols])
@@ -268,16 +254,29 @@
                     i = 6 * a + 2 * b + lb
                     pw1[half, i // 3, i % 3] = block
                 else:
-                    i = 2 * b + lb
-                    pw2[half, i // 2, i % 2] = block
+                    for yy in range(NY):
+                        pw2[half, 2 * b + lb, yy] = block[64 * yy : 64 * yy + 64]
+
+    def factors():
+        gt = dot_tn(zc_v[...], act_v[...])
+        pt = dot_tn(gz_v[...], t_v[...])
+        q_t = jnp.concatenate([gt[0:64], gt[64:96] + gt[96:128], pt[96:128]], axis=0)
+        q = q_t.T
+        for cc in range(NC):
+            for yy in range(NY):
+                for zp in range(NZ // 2):
+                    lo = 16 * (2 * zp * NY + yy) + 8 * cc
+                    hi = 16 * ((2 * zp + 1) * NY + yy) + 8 * cc
+                    tile = jnp.concatenate([q[lo : lo + 8], q[hi : hi + 8]], axis=0).astype(BF16)
+                    pw2[cc, 6, yy, 16 * zp : 16 * zp + 16, :] = tile
+                    pw2[cc, 7, yy, 16 * zp : 16 * zp + 16, :] = tile
 
     other = 1 - core
-    mate = (tm, x * NC + other)
 
     def core_copy(src, dst, i):
         return pltpu.make_async_remote_copy(
             src_ref=src, dst_ref=dst, send_sem=core_ss.at[i], recv_sem=core_rs.at[i],
-            device_id=mate, device_id_type=MESH,
+            device_id=(tm, x * NC + other), device_id_type=MESH,
         )
 
     core_copies = (
@@ -285,13 +284,15 @@
         core_copy(pw1.at[other, pl.ds(2, 2)], rc1.at[pl.ds(2, 2)], 1),
         core_copy(pw2.at[other], rc2, 2),
     )
-    for a in range(3):
-        space(a, other)
-        core_copies[a].start()
+    space(0, other)
+    core_copies[0].start()
+    space(1, other)
+    core_copies[1].start()
+    factors()
+    space(2, other)
+    core_copies[2].start()
     for a in range(3):
         space(a, core)
-
-    left, right, far = lax.rem(x + 3, NX), lax.rem(x + 1, NX), lax.rem(x + 2, NX)
 
     def x_copy(src, dst, to, i):
         return pltpu.make_async_remote_copy(
@@ -299,81 +300,109 @@
             device_id=(tm, to * NC + core), device_id_type=MESH,
         )
 
-    half_a, half_b = pl.ds(0, 128), pl.ds(128, 128)
-
-    def x_first(w, pw, rc, rel, sm, fin):
-        def add(chunk):
-            for s in range(pw.shape[2]):
-                sm[chunk, s] = (pw[core, chunk, s].astype(F32) + rc[chunk, s].astype(F32)).astype(BF16)
-
+    def y_copy(src, dst, to, i):
+        return pltpu.make_async_remote_copy(
+            src_ref=src, dst_ref=dst, send_sem=y_ss.at[i], recv_sem=y_rs.at[i],
+            device_id=(z * NY + to, clip), device_id_type=MESH,
+        )
+
+    def plus(a, b):
+        return (a.astype(F32) + b.astype(F32)).astype(BF16)
+
+    def halves1(ref, *at):
+        return [ref.at[(*at, slice(None), pl.ds(128 * h, 128))] for h in range(2)]
+
+    def halves2(ref, *at):
+        return [ref.at[(*at, pl.ds(4 * h, 4))] for h in range(2)]
+
+    def add1(chunk):
+        for s in range(3):
+            sum1[chunk, s] = plus(pw1[core, chunk, s], rc1[chunk, s])
+
+    def add2(chunk):
+        for s in range(8):
+            sum2[chunk, s] = plus(pw2[core, s, chunk], rc2[s, chunk])
+
+    def first(me, copy, halves, add, rel, sm, fin):
+        left, right, far = lax.rem(me + 3, 4), lax.rem(me + 1, 4), lax.rem(me + 2, 4)
         add(far)
-        to_l = x_copy(sm.at[far, :, half_a], rel.at[0], left, w + 0)
-        to_r = x_copy(sm.at[far, :, half_b], rel.at[1], right, w + 1)
-        to_l.start()
-        to_r.start()
+        a, b = halves(sm, far)
+        copies = [copy(a, rel.at[0], left, 0), copy(b, rel.at[1], right, 1)]
+        copies[0].start()
+        copies[1].start()
         add(left)
-        d_l = x_copy(sm.at[left, :, half_b], fin.at[1, :, half_b], left, w + 2)
-        d_l.start()
+        copies.append(copy(halves(sm, left)[1], halves(fin, 1)[1], left, 2))
+        copies[2].start()
         add(right)
-        d_r = x_copy(sm.at[right, :, half_a], fin.at[0, :, half_a], right, w + 3)
-        d_r.start()
-        add(x)
-        return [to_l, to_r, d_l, d_r]
-
-    def x_second(w, rel, sm, fin, copies):
-        n = sm.shape[1]
+        copies.append(copy(halves(sm, right)[0], halves(fin, 0)[0], right, 3))
+        copies[3].start()
+        add(me)
+        return copies
+
+    def second(me, copy, halves, relay, sm, fin, copies):
+        left, right = lax.rem(me + 3, 4), lax.rem(me + 1, 4)
         copies[0].wait_recv()
-        for s in range(n):
-            sm[left, s, 0:128] = (sm[left, s, 0:128].astype(F32) + rel[0, s].astype(F32)).astype(BF16)
-        s_l = x_copy(sm.at[left, :, half_a], fin.at[1, :, half_a], left, w + 4)
-        s_l.start()
+        relay(left, 0)
+        copies.append(copy(halves(sm, left)[0], halves(fin, 1)[0], left, 4))
+        copies[4].start()
         copies[1].wait_recv()
-        for s in range(n):
-            sm[right, s, 128:256] = (sm[right, s, 128:256].astype(F32) + rel[1, s].astype(F32)).astype(BF16)
-        s_r = x_copy(sm.at[right, :, half_b], fin.at[0, :, half_b], right, w + 5)
-        s_r.start()
-        return [s_l, s_r]
+        relay(right, 1)
+        copies.append(copy(halves(sm, right)[1], halves(fin, 0)[1], right, 5))
+        copies[5].start()
+
+    def relay1(chunk, h):
+        for s in range(3):
+            rows = slice(128 * h, 128 * h + 128)
+            sum1[chunk, s, rows] = plus(sum1[chunk, s, rows], rel1[h, s])
+
+    def relay2(chunk, h):
+        for s in range(4):
+            sum2[chunk, 4 * h + s] = plus(sum2[chunk, 4 * h + s], rel2[h, s])
 
     core_copies[0].wait_recv()
     core_copies[1].wait_recv()
-    first1 = x_first(0, pw1, rc1, rel1, sum1, fin1)
+    copies1 = first(x, x_copy, halves1, add1, rel1, sum1, fin1)
     core_copies[2].wait_recv()
-    first2 = x_first(6, pw2, rc2, rel2, sum2, fin2)
+    copies2 = first(y, y_copy, halves2, add2, rel2, sum2, fin2)
+
+    ld_ws.wait()
+    grad_x(0)
+
+    second(y, y_copy, halves2, relay2, sum2, fin2, copies2)
+    second(x, x_copy, halves1, relay1, sum1, fin1, copies1)
 
     grad_x(1)
 
-    second1 = x_second(0, rel1, sum1, fin1, first1)
-    second2 = x_second(6, rel2, sum2, fin2, first2)
-
-    def x_last(sm, fin, first, second, base):
-        for copy in first[2:] + second:
-            copy.wait_recv()
-        for s in range(sm.shape[1]):
-            tot = sm[x, s].astype(F32) + fin[0, s].astype(F32) + fin[1, s].astype(F32)
-            tot = tot.astype(BF16)
-            for yy in range(NY):
-                yb[yy, base + s] = tot[64 * yy : 64 * yy + 64]
-
-    x_last(sum1, fin1, first1, second1, 0)
-    x_last(sum2, fin2, first2, second2, 3)
-
-    y_copies = []
+    for copy in copies2[2:]:
+        copy.wait_recv()
+    for s in range(8):
+        last2[s] = (
+            sum2[y, s].astype(F32) + fin2[0, s].astype(F32) + fin2[1, s].astype(F32)
+        ).astype(BF16)
+    for d in range(1, NX):
+        to = lax.rem(x + d, NX)
+        copy = x_copy(last2.at[pl.ds(2 * to, 2)], got2.at[d - 1], to, 5 + d)
+        copy.start()
+        copies2.append(copy)
+    for copy in copies1[2:]:
+        copy.wait_recv()
+    for s in range(3):
+        tot = sum1[x, s].astype(F32) + fin1[0, s].astype(F32) + fin1[1, s].astype(F32)
+        tot = tot.astype(BF16)
+        for yy in range(NY):
+            last1[yy, s] = tot[64 * yy : 64 * yy + 64]
     for d in range(1, NY):
         to = lax.rem(y + d, NY)
-        copy = pltpu.make_async_remote_copy(
-            src_ref=yb.at[to], dst_ref=ry.at[d - 1],
-            send_sem=y_ss.at[d - 1], recv_sem=y_rs.at[d - 1],
-            device_id=(z * NY + to, clip), device_id_type=MESH,
-        )
+        copy = y_copy(last1.at[to], got1.at[d - 1], to, 5 + d)
         copy.start()
-        y_copies.append(copy)
-    for copy in y_copies:
+        copies1.append(copy)
+    for copy in copies2[6:] + copies1[6:]:
         copy.wait_recv()
     tots = []
     for s in range(5):
-        tot = yb[y, s].astype(F32)
-        for d in range(NY - 1):
-            tot = tot + ry[d, s].astype(F32)
+        tot = (last1[y, s] if s < 3 else last2[2 * x + s - 3]).astype(F32)
+        for d in range(3):
+            tot = tot + (got1[d, s] if s < 3 else got2[d, s - 3]).astype(F32)
         tots.append(tot)
     blank = jnp.zeros((8, 128), F32)
     for zz in range(NZ):
@@ -398,21 +427,39 @@
     tot = zs[z].astype(F32)
     for d in range(NZ - 1):
         tot = tot + rz[d].astype(F32)
-    fs[...] = (tot * SCALE).astype(BF16)
-    ra[clip] = fs[...]
+    ra[core, x] = (tot * SCALE).astype(BF16)
 
     g_copies = []
-    for d in range(1, NG):
+    for d in range(1, NX):
         copy = pltpu.make_async_remote_copy(
-            src_ref=fs, dst_ref=ra.at[clip],
+            src_ref=ra.at[core, x], dst_ref=ra.at[core, x],
             send_sem=g_ss.at[d - 1], recv_sem=g_rs.at[d - 1],
-            device_id=(tm, lax.rem(clip + d, NG)), device_id_type=MESH,
+            device_id=(tm, lax.rem(x + d, NX) * NC + core), device_id_type=MESH,
         )
         copy.start()
         g_copies.append(copy)
     for copy in g_copies:
         copy.wait_recv()
-
+    copy = pltpu.make_async_remote_copy(
+        src_ref=ra.at[core], dst_ref=ra.at[core],
+        send_sem=g_ss.at[NX - 1], recv_sem=g_rs.at[NX - 1],
+        device_id=(tm, x * NC + other), device_id_type=MESH,
+    )
+    copy.start()
+    g_copies.append(copy)
+    copy.wait_recv()
+
+    halo.wait_send()
+    for copy in [*core_copies, *copies1, *copies2, *z_copies, *g_copies]:
+        copy.wait_send()
+    sent = ab_v.at[pl.ds(0, NT - 1)]
+    pltpu.make_async_copy(sent, sent, a2a_ss).wait()
+    pltpu.make_async_copy(out_hbm, out_hbm, a2a_rs).wait()
+
+
+def finish(raw, ra, pj_ref, out_hbm, space_ref, time_ref, proj_ref, sem):
+    whole = pltpu.make_async_copy(raw, out_hbm, sem)
+    whole.start()
     for cc in range(NC):
         for i in range(18):
             a, b, lb = i // 6, i // 2 % 3, i % 2
@@ -420,24 +467,17 @@
                 xx, s = i // 3, i % 3
             else:
                 xx, s = (i - 12) // 2, 3 + i % 2
-            tile = ra[xx * NC + cc, 16 * (s // 2) : 16 * (s // 2) + 16].astype(F32)
+            tile = ra[cc, xx, 16 * (s // 2) : 16 * (s // 2) + 16].astype(F32)
             lo = 256 * cc + 128 * lb
             space_ref[3 * a + b, :, lo : lo + 128] = tile[8 * (s % 2) : 8 * (s % 2) + 8]
-    qs = jnp.concatenate([ra[3 * NC + cc, 16:32].astype(F32)[8:16] for cc in range(NC)], axis=0)
-    q_lane = iota((16, 128), 1)
+    qs = jnp.concatenate([ra[cc, 3, 16:32].astype(F32)[8:16] for cc in range(NC)], axis=0)
+    qs = qs.astype(BF16)
     for k in range(3):
-        time_ref[k] = dot(jnp.where(q_lane // 32 == k, qs, 0.0).astype(BF16), p3_v[...])
+        take = ones_where(iota((128, LAT), 0) == iota((128, LAT), 1) + 32 * k)
+        time_ref[k] = dot(dot(qs, take).astype(BF16), pj_ref[...])
     take = ones_where(iota((128, LAT), 0) == iota((128, LAT), 1) + 96)
-    proj_ref[...] = dot(qs.astype(BF16), take)
-
-    halo.wait_send()
-    for copy in core_copies:
-        copy.wait_send()
-    for copy in first1 + first2 + second1 + second2 + y_copies + z_copies + g_copies:
-        copy.wait_send()
-    sent = ab_v.at[pl.ds(0, NT - 1)]
-    pltpu.make_async_copy(sent, sent, a2a_ss).wait()
-    pltpu.make_async_copy(out_hbm, out_hbm, a2a_rs).wait()
+    proj_ref[...] = dot(qs, take)
+    whole.wait()
 
 
 def per_device(block_input, pre_act, time_out, w_space, w_time, proj, codes, cotan, lengths):
@@ -452,45 +492,54 @@
         cotan.reshape(ROWS, LAT),
         lengths,
     )
-    anywhere = pl.BlockSpec(memory_space=pl.ANY)
+    hbm = pl.BlockSpec(memory_space=pltpu.HBM)
+    held = [pltpu.with_memory_space_constraint(a, pltpu.HBM) for a in args]
     vmem = pl.BlockSpec(memory_space=pltpu.VMEM)
     dma = pltpu.SemaphoreType.DMA
     v = pltpu.VMEM
+    limit = 40 * 1024 * 1024
+    raw, sums = pl.pallas_call(
+        kernel,
+        out_shape=(pltpu.VMEM((2 * NT, 16, CIN), BF16), pltpu.VMEM((NC, NX, 48, 128), BF16)),
+        in_specs=[hbm] * 9,
+        out_specs=(vmem, vmem),
+        scratch_shapes=[
+            v((ROWS, CIN), BF16), v((ROWS, CMID), BF16), v((ROWS, CMID), BF16),
+            v((9, CIN, CMID), BF16), v((3, CMID, CMID), BF16), v((LAT, CMID), BF16),
+            v((FR * 16, 16), I32), v((ROWS, LAT), BF16), pltpu.SMEM((NG,), I32),
+            v((128, CMID), BF16), v((ROWS, 128), BF16), v((ROWS, 128), BF16),
+            v((CMID, 128), BF16), v((ROWS, CMID), BF16), v((ROWS, CMID), F32),
+            v((3, ROWS, CMID), BF16), v((768, ROWS), BF16),
+            v((CELLS, 128), BF16), v((CELLS, 128), BF16), v((NT, 2, 16, CIN), BF16),
+            v((NC, NX, 3, 256, 128), BF16), v((NC, 8, NY, 64, 128), BF16),
+            v((NX, 3, 256, 128), BF16), v((8, NY, 64, 128), BF16),
+            v((2, 3, 128, 128), BF16), v((2, 4, 64, 128), BF16),
+            v((NX, 3, 256, 128), BF16), v((NY, 8, 64, 128), BF16),
+            v((2, 3, 256, 128), BF16), v((2, 8, 64, 128), BF16),
+            v((NY, 3, 64, 128), BF16), v((8, 64, 128), BF16),
+            v((NY - 1, 3, 64, 128), BF16), v((NX - 1, 2, 64, 128), BF16),
+            v((NZ, 48, 128), BF16), v((NZ - 1, 48, 128), BF16),
+            dma((10,)), dma(()), dma(()), dma(()), dma(()),
+            dma((3,)), dma((3,)), dma((9,)), dma((9,)), dma((9,)), dma((9,)),
+            dma((NZ - 1,)), dma((NZ - 1,)), dma((NX,)), dma((NX,)),
+        ],
+        compiler_params=pltpu.CompilerParams(
+            collective_id=0, has_side_effects=True, vmem_limit_bytes=limit
+        ),
+    )(*held)
     out, space, time, projg = pl.pallas_call(
-        kernel,
+        finish,
         out_shape=(
             jax.ShapeDtypeStruct((2 * NT, 16, CIN), BF16),
             jax.ShapeDtypeStruct((9, 8, CMID), F32),
             jax.ShapeDtypeStruct((3, 16, CMID), F32),
             jax.ShapeDtypeStruct((16, LAT), F32),
         ),
-        in_specs=[anywhere] * 8 + [pl.BlockSpec(memory_space=pltpu.SMEM)],
-        out_specs=(anywhere, vmem, vmem, vmem),
-        scratch_shapes=[
-            v((ROWS, CIN), BF16), v((ROWS, CMID), BF16), v((ROWS, CMID), BF16),
-            v((9, CIN, CMID), BF16), v((3, CMID, CMID), BF16), v((LAT, CMID), BF16),
-            v((FR * 16, 16), I32), v((ROWS, LAT), BF16),
-            v((128, CMID), BF16), v((ROWS, 128), BF16), v((ROWS, 128), BF16),
-            v((128, CMID), BF16), v((ROWS, CMID), BF16), v((ROWS, CMID), F32),
-            v((3, ROWS, CMID), BF16), v((768, ROWS), BF16),
-            v((CELLS, 128), BF16), v((CELLS, 128), BF16), v((NT, 2, 16, CIN), BF16),
-            v((NC, NX, 3, 256, 128), BF16), v((NC, NX, 2, 256, 128), BF16),
-            v((NX, 3, 256, 128), BF16), v((NX, 2, 256, 128), BF16),
-            v((2, 3, 128, 128), BF16), v((2, 2, 128, 128), BF16),
-            v((NX, 3, 256, 128), BF16), v((NX, 2, 256, 128), BF16),
-            v((2, 3, 256, 128), BF16), v((2, 2, 256, 128), BF16),
-            v((NY, 5, 64, 128), BF16), v((NY - 1, 5, 64, 128), BF16),
-            v((NZ, 48, 128), BF16), v((NZ - 1, 48, 128), BF16),
-            v((48, 128), BF16), v((NG, 48, 128), BF16),
-            dma((9,)), dma(()), dma(()), dma(()), dma(()),
-            dma((3,)), dma((3,)), dma((12,)), dma((12,)),
-            dma((NY - 1,)), dma((NY - 1,)), dma((NZ - 1,)), dma((NZ - 1,)),
-            dma((NG - 1,)), dma((NG - 1,)),
-        ],
-        compiler_params=pltpu.CompilerParams(
-            collective_id=0, has_side_effects=True, vmem_limit_bytes=56 * 1024 * 1024
-        ),
-    )(*args)
+        in_specs=[vmem, vmem, vmem],
+        out_specs=(hbm, vmem, vmem, vmem),
+        scratch_shapes=[dma(())],
+        compiler_params=pltpu.CompilerParams(vmem_limit_bytes=8 * 1024 * 1024),
+    )(raw, sums, args[5])
     return (
         out.reshape(1, FR * NT, 8, CIN),
         space.reshape(3, 3, 8, CMID).transpose(2, 0, 1, 3),

time: 57.6 us -> 49.2 us (0.85)
  local copies, waits for them, and re-layouts: 6.28 us -> 0.01 us
  Pallas kernels: 50.4 us -> 48.5 us
    unnamed x4 -> x2, local copies, waits for them, and re-layouts: 6.28 us -> 0.01 us
    pallas_call x1 -> x2, Pallas kernels: 50.4 us -> 48.5 us  [the longest x1 47 us: per_device(): pl.pallas_call(kernel, out_shape=(pltpu.VMEM((2 * NT, 16, CIN), BF16), pl...]
where the time goes in v2:
time: 49.2 us; the launch traced here: 49.1 us
  Pallas kernels  48.5 us (99%)
  between operations  0.66 us (1%)
    pallas_call x1, Pallas kernels, per_device(): pl.pallas_call(kernel, out_shape=(pltpu.VMEM((2 * NT, 16, CIN), BF16), pl...  47 us
    pallas_call x1, Pallas kernels, per_device(): pl.pallas_call(finish, out_shape=(jax.ShapeDtypeStruct((2 * NT, 16, CIN),...  1.51 us

profile of v2, /device:TPU:1, one launch (start us, length us, event | category | flops | bytes accessed | tf_op | source)
XLA Modules:
  0.0 49.1 jit_solution(14493620770896830591)
XLA Ops:
  0.6 0.0 copy-start
  0.6 47.0 %shard_map.120 = (bf16[64,16,256]{2,1,0:T(8,128)(2,1)S(1)}, bf16[2,4,48,128]{3,2,1,0:T(8,128)(2,1)S(1)}) custom-call(bf16[1024,256]{1,0:T(8,128)(2,1)} %bitcast.21, bf16[1024,512]{1,0:T(8,128)(2,1)} %bitcast.19, bf16[1024,512]{1,0:T(8,128)(2,1)} %bitcast.20, bf16[9,256,512]{2,1,0:T(8,128)(2,1)} %bitcast.17, bf16[3,512,512]{2,1,0:T(8,128)(2,1)} %bitcast.18, ...), custom_call_target="tpu_custom_call" | custom-call | tf_op jit(solution)/shard_map/pallas_call | solution.py:501
  47.6 0.0 copy-done
  47.6 1.5 %shard_map.121 = (bf16[64,16,256]{2,1,0:T(8,128)(2,1)}, f32[9,8,512]{2,1,0:T(8,128)}, f32[3,16,512]{2,1,0:T(8,128)}, f32[16,18]{1,0:T(8,128)}) custom-call(bf16[64,16,256]{2,1,0:T(8,128)(2,1)S(1)} %get-tuple-element.10.raw, bf16[2,4,48,128]{3,2,1,0:T(8,128)(2,1)S(1)} %get-tuple-element.11.ra, bf16[18,512]{1,0:T(8,128)(2,1)S(1)} %bitcast.16), custom_call_target="tpu_custom_call" | custom-call | tf_op jit(solution)/shard_map/pallas_call | solution.py:530
Async XLA Ops:
  0.6 47.0 %copy-start = (bf16[512,18]{0,1:T(8,128)(2,1)S(1)}, bf16[512,18]{0,1:T(8,128)(2,1)}, u32[]{:S(2)}) copy-start(bf16[512,18]{0,1:T(8,128)(2,1)} %param.14) | copy-start | bytes 55300

commit v3 on v2

--- a/solution.py
+++ b/solution.py
@@ -204,9 +204,10 @@
             )
             ab_v[t, fp] = both.astype(BF16)
 
+    def send_x(fp):
         @pl.loop(1, NT)
         def _(d):
-            to = lax.rem(tm + d, NT)
+            to = lax.rem(z + d % NZ, NZ) * NY + lax.rem(y + d // NZ, NY)
             pltpu.make_async_remote_copy(
                 src_ref=ab_v.at[to, fp], dst_ref=out_hbm.at[2 * tm + fp],
                 send_sem=a2a_ss, recv_sem=a2a_rs,
@@ -367,11 +368,13 @@
 
     ld_ws.wait()
     grad_x(0)
+    send_x(0)
 
     second(y, y_copy, halves2, relay2, sum2, fin2, copies2)
     second(x, x_copy, halves1, relay1, sum1, fin1, copies1)
 
     grad_x(1)
+    send_x(1)
 
     for copy in copies2[2:]:
         copy.wait_recv()

time: 49.2 us -> 48.1 us (0.978)
  Pallas kernels: 48.5 us -> 47.3 us
    pallas_call x1, Pallas kernels: 47 us -> 45.8 us  [per_device(): pl.pallas_call(kernel, out_shape=(pltpu.VMEM((2 * NT, 16, CIN), BF16), pl...]
where the time goes in v3:
time: 48.1 us; the launch traced here: 48 us
  Pallas kernels  47.3 us (98%)
  between operations  0.66 us (1%)
    pallas_call x1, Pallas kernels, per_device(): pl.pallas_call(kernel, out_shape=(pltpu.VMEM((2 * NT, 16, CIN), BF16), pl...  45.8 us
    pallas_call x1, Pallas kernels, per_device(): pl.pallas_call(finish, out_shape=(jax.ShapeDtypeStruct((2 * NT, 16, CIN),...  1.51 us

profile of v3, /device:TPU:1, one launch (start us, length us, event | category | flops | bytes accessed | tf_op | source)
XLA Modules:
  0.0 48.0 jit_solution(18419554145763036035)
XLA Ops:
  0.6 0.0 copy-start
  0.6 45.8 %shard_map.120 = (bf16[64,16,256]{2,1,0:T(8,128)(2,1)S(1)}, bf16[2,4,48,128]{3,2,1,0:T(8,128)(2,1)S(1)}) custom-call(bf16[1024,256]{1,0:T(8,128)(2,1)} %bitcast.21, bf16[1024,512]{1,0:T(8,128)(2,1)} %bitcast.19, bf16[1024,512]{1,0:T(8,128)(2,1)} %bitcast.20, bf16[9,256,512]{2,1,0:T(8,128)(2,1)} %bitcast.17, bf16[3,512,512]{2,1,0:T(8,128)(2,1)} %bitcast.18, ...), custom_call_target="tpu_custom_call" | custom-call | tf_op jit(solution)/shard_map/pallas_call | solution.py:504
  46.5 0.0 copy-done
  46.5 1.5 %shard_map.121 = (bf16[64,16,256]{2,1,0:T(8,128)(2,1)}, f32[9,8,512]{2,1,0:T(8,128)}, f32[3,16,512]{2,1,0:T(8,128)}, f32[16,18]{1,0:T(8,128)}) custom-call(bf16[64,16,256]{2,1,0:T(8,128)(2,1)S(1)} %get-tuple-element.10.raw, bf16[2,4,48,128]{3,2,1,0:T(8,128)(2,1)S(1)} %get-tuple-element.11.ra, bf16[18,512]{1,0:T(8,128)(2,1)S(1)} %bitcast.16), custom_call_target="tpu_custom_call" | custom-call | tf_op jit(solution)/shard_map/pallas_call | solution.py:533
Async XLA Ops:
  0.6 45.8 %copy-start = (bf16[512,18]{0,1:T(8,128)(2,1)S(1)}, bf16[512,18]{0,1:T(8,128)(2,1)}, u32[]{:S(2)}) copy-start(bf16[512,18]{0,1:T(8,128)(2,1)} %param.14) | copy-start | bytes 55300

commit v4 on v3

--- a/solution.py
+++ b/solution.py
@@ -433,24 +433,16 @@
     ra[core, x] = (tot * SCALE).astype(BF16)
 
     g_copies = []
-    for d in range(1, NX):
+    for d in (4, 5, 3, 2, 6, 7, 1):
         copy = pltpu.make_async_remote_copy(
             src_ref=ra.at[core, x], dst_ref=ra.at[core, x],
             send_sem=g_ss.at[d - 1], recv_sem=g_rs.at[d - 1],
-            device_id=(tm, lax.rem(x + d, NX) * NC + core), device_id_type=MESH,
+            device_id=(tm, lax.rem(clip + d, NG)), device_id_type=MESH,
         )
         copy.start()
         g_copies.append(copy)
     for copy in g_copies:
         copy.wait_recv()
-    copy = pltpu.make_async_remote_copy(
-        src_ref=ra.at[core], dst_ref=ra.at[core],
-        send_sem=g_ss.at[NX - 1], recv_sem=g_rs.at[NX - 1],
-        device_id=(tm, x * NC + other), device_id_type=MESH,
-    )
-    copy.start()
-    g_copies.append(copy)
-    copy.wait_recv()
 
     halo.wait_send()
     for copy in [*core_copies, *copies1, *copies2, *z_copies, *g_copies]:
@@ -524,7 +516,7 @@
             v((NZ, 48, 128), BF16), v((NZ - 1, 48, 128), BF16),
             dma((10,)), dma(()), dma(()), dma(()), dma(()),
             dma((3,)), dma((3,)), dma((9,)), dma((9,)), dma((9,)), dma((9,)),
-            dma((NZ - 1,)), dma((NZ - 1,)), dma((NX,)), dma((NX,)),
+            dma((NZ - 1,)), dma((NZ - 1,)), dma((NG - 1,)), dma((NG - 1,)),
         ],
         compiler_params=pltpu.CompilerParams(
             collective_id=0, has_side_effects=True, vmem_limit_bytes=limit

time: 48.1 us -> 46.9 us (0.975)
  Pallas kernels: 47.3 us -> 46.1 us
    pallas_call x1, Pallas kernels: 45.8 us -> 44.6 us  [per_device(): pl.pallas_call(kernel, out_shape=(pltpu.VMEM((2 * NT, 16, CIN), BF16), pl...]
where the time goes in v4:
time: 46.9 us; the launch traced here: 46.8 us
  Pallas kernels  46.1 us (98%)
  between operations  0.66 us (1%)
    pallas_call x1, Pallas kernels, per_device(): pl.pallas_call(kernel, out_shape=(pltpu.VMEM((2 * NT, 16, CIN), BF16), pl...  44.6 us
    pallas_call x1, Pallas kernels, per_device(): pl.pallas_call(finish, out_shape=(jax.ShapeDtypeStruct((2 * NT, 16, CIN),...  1.51 us

profile of v4, /device:TPU:1, one launch (start us, length us, event | category | flops | bytes accessed | tf_op | source)
XLA Modules:
  0.0 46.8 jit_solution(2884641555046892925)
XLA Ops:
  0.6 0.0 copy-start
  0.6 44.6 %shard_map.120 = (bf16[64,16,256]{2,1,0:T(8,128)(2,1)S(1)}, bf16[2,4,48,128]{3,2,1,0:T(8,128)(2,1)S(1)}) custom-call(bf16[1024,256]{1,0:T(8,128)(2,1)} %bitcast.21, bf16[1024,512]{1,0:T(8,128)(2,1)} %bitcast.19, bf16[1024,512]{1,0:T(8,128)(2,1)} %bitcast.20, bf16[9,256,512]{2,1,0:T(8,128)(2,1)} %bitcast.17, bf16[3,512,512]{2,1,0:T(8,128)(2,1)} %bitcast.18, ...), custom_call_target="tpu_custom_call" | custom-call | tf_op jit(solution)/shard_map/pallas_call | solution.py:496
  45.3 0.0 copy-done
  45.3 1.5 %shard_map.121 = (bf16[64,16,256]{2,1,0:T(8,128)(2,1)}, f32[9,8,512]{2,1,0:T(8,128)}, f32[3,16,512]{2,1,0:T(8,128)}, f32[16,18]{1,0:T(8,128)}) custom-call(bf16[64,16,256]{2,1,0:T(8,128)(2,1)S(1)} %get-tuple-element.10.raw, bf16[2,4,48,128]{3,2,1,0:T(8,128)(2,1)S(1)} %get-tuple-element.11.ra, bf16[18,512]{1,0:T(8,128)(2,1)S(1)} %bitcast.16), custom_call_target="tpu_custom_call" | custom-call | tf_op jit(solution)/shard_map/pallas_call | solution.py:525
Async XLA Ops:
  0.6 44.6 %copy-start = (bf16[512,18]{0,1:T(8,128)(2,1)S(1)}, bf16[512,18]{0,1:T(8,128)(2,1)}, u32[]{:S(2)}) copy-start(bf16[512,18]{0,1:T(8,128)(2,1)} %param.14) | copy-start | bytes 55300
